TPU v7x, 256 devices: a whole 4x4x8 slice. The times are simulated.
256 devices in a mesh: seq: 128 (over z, y, x_hi, core), chan: 2 (over x_lo).
Axes of the slice: x: 4 (x_hi: 2, x_lo: 2; x = x_hi * 2 + x_lo), y: 4, z: 8, core: 2. Of those that a mesh axis runs over, the one named last changes fastest.
Arguments:
- signal: bfloat16 [128, 65536], P('chan', 'seq'), may hold values from -6 to 6
- cotangent: bfloat16 [128, 65536], P('chan', 'seq'), may hold values from -18 to 18
- filters: bfloat16 [64, 65536], P(None, 'seq'), may hold values from -1.6 to 1.6
- skip: float32 [128], P('chan'), may hold values from -4 to 4
Outputs:
- signal_grad: bfloat16 [128, 65536], P('chan', 'seq')
- filter_grad: float32 [64, 65536], P('chan', 'seq')
- skip_grad: float32 [128], P('chan')
All inputs are finite; a program needn't handle non-finite values.
Results may differ from a plain program's by a relative error of at most 0.013.
Values may be sent and summed in bfloat16 or wider, within the bound.
A program may use at most 64 MiB of HBM per device.

v0:
```python
import math
import jax
import jax.numpy as jnp
from jax import lax
from jax.sharding import PartitionSpec as P


def shortened(shard):
    return jax.tree.map(lambda a: a.astype(jnp.bfloat16) if a.dtype == jnp.float32 else a, shard)


def counting(height):
    return jnp.arange(height, dtype=jnp.int32)


def row_order(devices):
    first_slot = counting(devices)
    second_slot = jnp.where(first_slot == 0, devices, 2 * devices - first_slot)
    return jnp.stack([first_slot, second_slot], axis=1).reshape(2 * devices)


def phase(left_idx, right_idx, period):
    product_idx = left_idx[:, None] * right_idx[None, :] % period
    angles = product_idx.astype(jnp.float32) * (2.0 * math.pi / period)
    return (jnp.cos(angles), jnp.sin(angles))


def rotate(real_part, imag_part, cosine, sine_tab, pattern, orient):
    real_cos = jnp.einsum(pattern, real_part, cosine, precision=lax.Precision.HIGHEST)
    real_sin = jnp.einsum(pattern, real_part, sine_tab, precision=lax.Precision.HIGHEST)
    imag_cos = jnp.einsum(pattern, imag_part, cosine, precision=lax.Precision.HIGHEST)
    imag_sin = jnp.einsum(pattern, imag_part, sine_tab, precision=lax.Precision.HIGHEST)
    return (real_cos - orient * imag_sin, imag_cos + orient * real_sin)


def twist(real_part, imag_part, cosine, sine_tab, orient):
    return (
        real_part * cosine - orient * imag_part * sine_tab,
        imag_part * cosine + orient * real_part * sine_tab,
    )


def split_length(length):
    return max((divisor for divisor in range(1, math.isqrt(length) + 1) if length % divisor == 0))


def local_forward(real_part, imag_part):
    channels, twins, length = real_part.shape
    slow_len = split_length(length)
    fast_len = length // slow_len
    real_part = real_part.reshape(channels, twins, slow_len, fast_len)
    imag_part = imag_part.reshape(channels, twins, slow_len, fast_len)
    cos_slow, sin_slow = phase(counting(slow_len), counting(slow_len), slow_len)
    real_part, imag_part = rotate(real_part, imag_part, cos_slow, sin_slow, "cjab,ak->cjkb", -1.0)
    cos_turn, sin_turn = phase(counting(slow_len), counting(fast_len), length)
    real_part, imag_part = twist(real_part, imag_part, cos_turn, sin_turn, -1.0)
    cos_fast, sin_fast = phase(counting(fast_len), counting(fast_len), fast_len)
    return rotate(real_part, imag_part, cos_fast, sin_fast, "cjkb,bl->cjkl", -1.0)


def local_inverse(real_part, imag_part):
    channels, twins, slow_len, fast_len = real_part.shape
    length = slow_len * fast_len
    cos_fast, sin_fast = phase(counting(fast_len), counting(fast_len), fast_len)
    real_part, imag_part = rotate(real_part, imag_part, cos_fast, sin_fast, "cjkl,lb->cjkb", 1.0)
    cos_turn, sin_turn = phase(counting(slow_len), counting(fast_len), length)
    real_part, imag_part = twist(real_part, imag_part, cos_turn, sin_turn, 1.0)
    cos_slow, sin_slow = phase(counting(slow_len), counting(slow_len), slow_len)
    real_part, imag_part = rotate(real_part, imag_part, cos_slow, sin_slow, "cjkb,ka->cjab", 1.0)
    return (real_part.reshape(channels, twins, length), imag_part.reshape(channels, twins, length))


def rows_forward(real_set, padded, offset, order):
    height = real_set.shape[1]
    cos_rows, sin_rows = phase(counting(height), order, 2 * height)
    real_vals = real_set.astype(jnp.float32)
    real_part = jnp.einsum("cpr,pk->ckr", real_vals, cos_rows, precision=lax.Precision.HIGHEST)
    imag_part = -jnp.einsum("cpr,pk->ckr", real_vals, sin_rows, precision=lax.Precision.HIGHEST)
    cos_turn, sin_turn = phase(order, offset + counting(real_set.shape[2]), padded)
    return twist(real_part, imag_part, cos_turn, sin_turn, -1.0)


def rows_inverse(real_part, imag_part, padded, offset, order):
    height = real_part.shape[1] // 2
    cos_turn, sin_turn = phase(order, offset + counting(real_part.shape[2]), padded)
    real_part, imag_part = twist(real_part, imag_part, cos_turn, sin_turn, 1.0)
    cos_rows, sin_rows = phase(order, counting(height), 2 * height)
    real_cos = jnp.einsum("ckr,kp->cpr", real_part, cos_rows, precision=lax.Precision.HIGHEST)
    imag_sin = jnp.einsum("ckr,kp->cpr", imag_part, sin_rows, precision=lax.Precision.HIGHEST)
    out_real = (real_cos - imag_sin) / padded
    return out_real


def local(signal, cotangent, filters, skip):
    channels, length = signal.shape
    devices = lax.axis_size("seq")
    offset = lax.axis_index("seq") * (length // devices)
    padded = 2 * length * devices
    order = row_order(devices)
    norm_factor = 1.0 / math.sqrt(length * devices)
    columns = (
        lax.all_to_all(
            signal.reshape(channels, 1, length), "seq", split_axis=2, concat_axis=1, tiled=True
        ),
        lax.all_to_all(
            cotangent.reshape(channels, 1, length), "seq", split_axis=2, concat_axis=1, tiled=True
        ),
        lax.all_to_all(
            filters.reshape(filters.shape[0], 1, length),
            "seq",
            split_axis=2,
            concat_axis=1,
            tiled=True,
        ),
    )
    row_spectra = [rows_forward(column_set, padded, offset, order) for column_set in columns]
    spread = (
        lax.all_to_all(
            row_spectra[0][0].astype(jnp.bfloat16), "seq", split_axis=1, concat_axis=2, tiled=True
        ).astype(jnp.float32),
        lax.all_to_all(
            row_spectra[0][1].astype(jnp.bfloat16), "seq", split_axis=1, concat_axis=2, tiled=True
        ).astype(jnp.float32),
        lax.all_to_all(
            row_spectra[1][0].astype(jnp.bfloat16), "seq", split_axis=1, concat_axis=2, tiled=True
        ).astype(jnp.float32),
        lax.all_to_all(
            row_spectra[1][1].astype(jnp.bfloat16), "seq", split_axis=1, concat_axis=2, tiled=True
        ).astype(jnp.float32),
        lax.all_to_all(
            row_spectra[2][0].astype(jnp.bfloat16), "seq", split_axis=1, concat_axis=2, tiled=True
        ).astype(jnp.float32),
        lax.all_to_all(
            row_spectra[2][1].astype(jnp.bfloat16), "seq", split_axis=1, concat_axis=2, tiled=True
        ).astype(jnp.float32),
    )
    signal_real, signal_imag = local_forward(spread[0], spread[1])
    cotan_real, cotan_imag = local_forward(spread[2], spread[3])
    filter_real, filter_imag = local_forward(spread[4], spread[5])
    conv_real = filter_real * cotan_real + filter_imag * cotan_imag
    conv_imag = filter_real * cotan_imag - filter_imag * cotan_real
    corr_real = signal_real * cotan_real + signal_imag * cotan_imag
    corr_imag = signal_real * cotan_imag - signal_imag * cotan_real
    cotan_val = cotangent.astype(jnp.float32)
    local_skip = jnp.sum(cotan_val * signal.astype(jnp.float32), axis=1)
    skip_grad = lax.psum(local_skip, "seq") * norm_factor
    back_conv_real, back_conv_imag = local_inverse(conv_real, conv_imag)
    back_corr_real, back_corr_imag = local_inverse(corr_real, corr_imag)
    arrived = (
        lax.all_to_all(
            shortened(back_conv_real), "seq", split_axis=2, concat_axis=1, tiled=True
        ).astype(back_conv_real.dtype),
        lax.all_to_all(
            shortened(back_conv_imag), "seq", split_axis=2, concat_axis=1, tiled=True
        ).astype(back_conv_imag.dtype),
        lax.all_to_all(
            shortened(back_corr_real), "seq", split_axis=2, concat_axis=1, tiled=True
        ).astype(back_corr_real.dtype),
        lax.all_to_all(
            shortened(back_corr_imag), "seq", split_axis=2, concat_axis=1, tiled=True
        ).astype(back_corr_imag.dtype),
    )
    time_conv = rows_inverse(arrived[0], arrived[1], padded, offset, order)
    time_corr = rows_inverse(arrived[2], arrived[3], padded, offset, order)
    placed = (
        lax.all_to_all(shortened(time_conv), "seq", split_axis=1, concat_axis=2, tiled=True).astype(
            time_conv.dtype
        ),
        lax.all_to_all(shortened(time_corr), "seq", split_axis=1, concat_axis=2, tiled=True).astype(
            time_corr.dtype
        ),
    )
    conv_time = placed[0].reshape(channels, length)
    filter_grad = (
        lax.psum_scatter(
            placed[1].reshape(channels, length).astype(jnp.bfloat16),
            "chan",
            scatter_dimension=0,
            tiled=True,
        ).astype(jnp.float32)
        * norm_factor
    )
    signal_grad = (conv_time + skip[:, None] * cotan_val).astype(jnp.bfloat16)
    return (signal_grad, filter_grad, skip_grad)


def solution(mesh):
    in_specs = (P("chan", "seq"), P("chan", "seq"), P(None, "seq"), P("chan"))
    out_specs = (P("chan", "seq"), P("chan", "seq"), P("chan"))
    return jax.shard_map(local, mesh=mesh, in_specs=in_specs, out_specs=out_specs, check_vma=False)
```

profile of v0, /device:TPU:1, one launch (start us, length us, event | category | flops | bytes accessed | tf_op | source)
XLA Modules:
  0.0 670.9 jit_solution(16680134016253449366)
XLA Ops:
  7.2 1.0 copy.333
  8.7 1.5 reduce
  10.9 16.4 %all-to-all-start.9 = ((bf16[128,2,128]{2,1,0:T(2,128)(2,1)}), bf16[128,2,128]{2,1,0:T(2,128)(2,1)S(1)}, u32[]{:S(2)}, u32[]{:S(2)}) async-start(bf16[128,2,128]{2,1,0:T(2,128)(2,1)} %reshape.263), calls=%async_computation.9 | async-start | bytes 131072 | tf_op jit(solution)/shard_map/all_to_all | solution.py:102
  28.4 1.5 reduce.1
  30.9 1.5 reduce.2
  33.3 5.7 all-to-all-done.9
  39.0 8.0 %all-to-all-start.3 = ((bf16[128,2,128]{2,1,0:T(2,128)(2,1)}), bf16[128,2,128]{2,1,0:T(2,128)(2,1)S(1)}, u32[]{:S(2)}, u32[]{:S(2)}) async-start(bf16[128,2,128]{2,1,0:T(2,128)(2,1)} %reshape.253), calls=%async_computation.3 | async-start | bytes 131072 | tf_op jit(solution)/shard_map/all_to_all | solution.py:105
  47.3 0.8 convolution_negate_fusion
  48.9 9.9 %all-to-all-done.3 = bf16[128,2,128]{2,1,0:T(2,128)(2,1)S(1)} async-done(((bf16[128,2,128]{2,1,0:T(2,128)(2,1)}), bf16[128,2,128]{2,1,0:T(2,128)(2,1)S(1)}, u32[]{:S(2)}, u32[]{:S(2)}) %all-to-all-start.3) | async-done | bytes 65568 | tf_op jit(solution)/shard_map/all_to_all | solution.py:105
  58.7 6.5 all-to-all-start
  67.1 10.0 %all-to-all-done = bf16[128,2,128]{2,1,0:T(2,128)(2,1)S(1)} async-done(((bf16[128,2,128]{2,1,0:T(2,128)(2,1)}), bf16[128,2,128]{2,1,0:T(2,128)(2,1)S(1)}, u32[]{:S(2)}, u32[]{:S(2)}) %all-to-all-start) | async-done | bytes 65568 | tf_op jit(solution)/shard_map/all_to_all | solution.py:108
  78.1 0.9 fusion.97
  79.2 0.9 reshape.255
  80.1 6.2 all-to-all-start.4
  86.5 0.9 reshape.257
  87.4 12.1 %all-to-all-done.4 = bf16[128,2,256]{2,1,0:T(2,128)(2,1)S(1)} async-done(((bf16[128,2,256]{2,1,0:T(2,128)(2,1)}), bf16[128,2,256]{2,1,0:T(2,128)(2,1)S(1)}, u32[]{:S(2)}, u32[]{:S(2)}) %all-to-all-start.4) | async-done | bytes 131104 | tf_op jit(solution)/shard_map/all_to_all | solution.py:124
  99.4 6.3 all-to-all-start.5
  106.5 0.9 reshape.251
  107.4 11.4 %all-to-all-done.5 = bf16[128,2,256]{2,1,0:T(2,128)(2,1)S(1)} async-done(((bf16[128,2,256]{2,1,0:T(2,128)(2,1)}), bf16[128,2,256]{2,1,0:T(2,128)(2,1)S(1)}, u32[]{:S(2)}, u32[]{:S(2)}) %all-to-all-start.5) | async-done | bytes 131104 | tf_op jit(solution)/shard_map/all_to_all | solution.py:127
  118.8 6.6 all-to-all-start.1
  127.0 0.9 reshape.249
  128.1 0.9 reshape.265
  129.1 0.9 reshape.267
  131.4 7.1 %all-to-all-done.1 = bf16[128,2,256]{2,1,0:T(2,128)(2,1)S(1)} async-done(((bf16[128,2,256]{2,1,0:T(2,128)(2,1)}), bf16[128,2,256]{2,1,0:T(2,128)(2,1)S(1)}, u32[]{:S(2)}, u32[]{:S(2)}) %all-to-all-start.1) | async-done | bytes 131104 | tf_op jit(solution)/shard_map/all_to_all | solution.py:130
  138.5 6.8 %all-to-all-start.2 = ((bf16[128,2,256]{2,1,0:T(2,128)(2,1)}), bf16[128,2,256]{2,1,0:T(2,128)(2,1)S(1)}, u32[]{:S(2)}, u32[]{:S(2)}) async-start(bf16[128,2,256]{2,1,0:T(2,128)(2,1)} %reshape.249), calls=%async_computation.2 | async-start | bytes 262144 | tf_op jit(solution)/shard_map/all_to_all | solution.py:133
  147.0 11.2 %all-to-all-done.2 = bf16[128,2,256]{2,1,0:T(2,128)(2,1)S(1)} async-done(((bf16[128,2,256]{2,1,0:T(2,128)(2,1)}), bf16[128,2,256]{2,1,0:T(2,128)(2,1)S(1)}, u32[]{:S(2)}, u32[]{:S(2)}) %all-to-all-start.2) | async-done | bytes 131104 | tf_op jit(solution)/shard_map/all_to_all | solution.py:133
  158.2 6.3 all-to-all-start.11
  165.8 11.8 %all-to-all-done.11 = bf16[128,2,256]{2,1,0:T(2,128)(2,1)S(1)} async-done(((bf16[128,2,256]{2,1,0:T(2,128)(2,1)}), bf16[128,2,256]{2,1,0:T(2,128)(2,1)S(1)}, u32[]{:S(2)}, u32[]{:S(2)}) %all-to-all-start.11) | async-done | bytes 131104 | tf_op jit(solution)/shard_map/all_to_all | solution.py:121
  177.6 7.7 %all-to-all-start.10 = ((bf16[128,2,256]{2,1,0:T(2,128)(2,1)}), bf16[128,2,256]{2,1,0:T(2,128)(2,1)}, u32[]{:S(2)}, u32[]{:S(2)}) async-start(bf16[128,2,256]{2,1,0:T(2,128)(2,1)} %reshape.267), calls=%async_computation.10 | async-start | bytes 262144 | tf_op jit(solution)/shard_map/all_to_all | solution.py:118
  185.8 1.2 convolution_multiply_fusion.1
  187.4 10.2 %all-to-all-done.10 = bf16[128,2,256]{2,1,0:T(2,128)(2,1)} async-done(((bf16[128,2,256]{2,1,0:T(2,128)(2,1)}), bf16[128,2,256]{2,1,0:T(2,128)(2,1)}, u32[]{:S(2)}, u32[]{:S(2)}) %all-to-all-start.10) | async-done | bytes 131104 | tf_op jit(solution)/shard_map/all_to_all | solution.py:118
  197.6 1.1 reshape.268
  210.5 1.2 multiply_subtract_fusion.1
  216.4 0.9 multiply_subtract_fusion
  217.3 0.8 fusion.38
  218.2 0.9 fusion.11
  219.4 0.9 reshape.269
  220.3 6.6 all-to-all-start.12
  226.9 0.8 fusion.34
  227.7 0.9 fusion.10
  229.0 0.9 reshape.271
  229.8 10.1 %all-to-all-done.12 = bf16[128,2,256]{2,1,0:T(2,128)(2,1)S(1)} async-done(((bf16[128,2,256]{2,1,0:T(2,128)(2,1)}), bf16[128,2,256]{2,1,0:T(2,128)(2,1)S(1)}, u32[]{:S(2)}, u32[]{:S(2)}) %all-to-all-start.12) | async-done | bytes 131104 | tf_op jit(solution)/shard_map/all_to_all | solution.py:156
  239.9 6.2 all-to-all-start.13
  246.2 0.8 fusion.50
  247.0 0.9 fusion.13
  248.3 0.9 reshape.259
  249.1 10.2 %all-to-all-done.13 = bf16[128,2,256]{2,1,0:T(2,128)(2,1)S(1)} async-done(((bf16[128,2,256]{2,1,0:T(2,128)(2,1)}), bf16[128,2,256]{2,1,0:T(2,128)(2,1)S(1)}, u32[]{:S(2)}, u32[]{:S(2)}) %all-to-all-start.13) | async-done | bytes 131104 | tf_op jit(solution)/shard_map/all_to_all | solution.py:159
  259.3 6.6 all-to-all-start.6
  265.9 0.8 fusion.46
  266.8 0.9 fusion.12
  268.0 0.9 reshape.261
  270.8 8.2 %all-to-all-done.6 = bf16[128,2,256]{2,1,0:T(2,128)(2,1)S(1)} async-done(((bf16[128,2,256]{2,1,0:T(2,128)(2,1)}), bf16[128,2,256]{2,1,0:T(2,128)(2,1)S(1)}, u32[]{:S(2)}, u32[]{:S(2)}) %all-to-all-start.6) | async-done | bytes 131104 | tf_op jit(solution)/shard_map/all_to_all | solution.py:150
  279.0 6.2 all-to-all-start.7
  285.9 1.5 fusion.23
  287.4 1.5 fusion.18
  290.8 7.5 %all-to-all-done.7 = bf16[128,2,256]{2,1,0:T(2,128)(2,1)S(1)} async-done(((bf16[128,2,256]{2,1,0:T(2,128)(2,1)}), bf16[128,2,256]{2,1,0:T(2,128)(2,1)S(1)}, u32[]{:S(2)}, u32[]{:S(2)}) %all-to-all-start.7) | async-done | bytes 131104 | tf_op jit(solution)/shard_map/all_to_all | solution.py:153
  298.3 6.8 %all-to-all-start.14 = ((bf16[128,2,128]{2,1,0:T(2,128)(2,1)}), bf16[128,2,128]{2,1,0:T(2,128)(2,1)S(1)}, u32[]{:S(2)}, u32[]{:S(2)}) async-start(bf16[128,2,128]{2,1,0:T(2,128)(2,1)} %reshape.275), calls=%async_computation.14 | async-start | bytes 131072 | tf_op jit(solution)/shard_map/all_to_all | solution.py:169
  306.0 1.5 fusion.30
  307.6 1.6 fusion.19
  310.1 6.8 %all-to-all-done.14 = bf16[128,2,128]{2,1,0:T(2,128)(2,1)S(1)} async-done(((bf16[128,2,128]{2,1,0:T(2,128)(2,1)}), bf16[128,2,128]{2,1,0:T(2,128)(2,1)S(1)}, u32[]{:S(2)}, u32[]{:S(2)}) %all-to-all-start.14) | async-done | bytes 65568 | tf_op jit(solution)/shard_map/all_to_all | solution.py:169
  316.8 7.2 %all-to-all-start.8 = ((bf16[128,2,128]{2,1,0:T(2,128)(2,1)}), bf16[128,2,128]{2,1,0:T(2,128)(2,1)S(1)}, u32[]{:S(2)}, u32[]{:S(2)}) async-start(bf16[128,2,128]{2,1,0:T(2,128)(2,1)} %reshape.273), calls=%async_computation.8 | async-start | bytes 131072 | tf_op jit(solution)/shard_map/all_to_all | solution.py:166
  325.8 9.8 %all-to-all-done.8 = bf16[128,2,128]{2,1,0:T(2,128)(2,1)S(1)} async-done(((bf16[128,2,128]{2,1,0:T(2,128)(2,1)}), bf16[128,2,128]{2,1,0:T(2,128)(2,1)S(1)}, u32[]{:S(2)}, u32[]{:S(2)}) %all-to-all-start.8) | async-done | bytes 65568 | tf_op jit(solution)/shard_map/all_to_all | solution.py:166
  337.3 324.1 %psum.7 = f32[64]{0:T(128)S(1)} all-reduce(f32[64]{0:T(128)S(1)} %get-tuple-element.37), channel_id=1, replica_groups=mesh['seq'=128,'chan'=2] {'seq'}, use_global_device_ids=true, to_apply=%region_2.3 | all-reduce | flops 64 | bytes 512 | tf_op jit(solution)/shard_map/psum | solution.py:146
  661.9 0.9 copy.379
  (145 shorter events, 44.4 us)
Async XLA Ops:
  10.9 28.1 %all-to-all-start.9 = ((bf16[128,2,128]{2,1,0:T(2,128)(2,1)}), bf16[128,2,128]{2,1,0:T(2,128)(2,1)S(1)}, u32[]{:S(2)}, u32[]{:S(2)}) async-start(bf16[128,2,128]{2,1,0:T(2,128)(2,1)} %reshape.263), calls=%async_computation.9 | async-start | bytes 131072 | tf_op jit(solution)/shard_map/all_to_all | solution.py:102
  27.4 0.8 copy-start.1
  27.6 50.5 %copy-start.7 = (s32[256]{0:T(256)}, s32[256]{0:T(256)S(1)}, u32[]{:S(2)}) copy-start(s32[256]{0:T(256)S(1)} %mul.1168) | copy-start | bytes 3076
  29.9 0.8 copy-start.6
  39.0 19.7 %all-to-all-start.3 = ((bf16[128,2,128]{2,1,0:T(2,128)(2,1)}), bf16[128,2,128]{2,1,0:T(2,128)(2,1)S(1)}, u32[]{:S(2)}, u32[]{:S(2)}) async-start(bf16[128,2,128]{2,1,0:T(2,128)(2,1)} %reshape.253), calls=%async_computation.3 | async-start | bytes 131072 | tf_op jit(solution)/shard_map/all_to_all | solution.py:105
  58.7 18.4 %all-to-all-start = ((bf16[128,2,128]{2,1,0:T(2,128)(2,1)}), bf16[128,2,128]{2,1,0:T(2,128)(2,1)S(1)}, u32[]{:S(2)}, u32[]{:S(2)}) async-start(bf16[128,2,128]{2,1,0:T(2,128)(2,1)} %reshape.247), calls=%async_computation | async-start | bytes 131072 | tf_op jit(solution)/shard_map/all_to_all | solution.py:108
  80.1 19.3 %all-to-all-start.4 = ((bf16[128,2,256]{2,1,0:T(2,128)(2,1)}), bf16[128,2,256]{2,1,0:T(2,128)(2,1)S(1)}, u32[]{:S(2)}, u32[]{:S(2)}) async-start(bf16[128,2,256]{2,1,0:T(2,128)(2,1)} %reshape.255), calls=%async_computation.4 | async-start | bytes 262144 | tf_op jit(solution)/shard_map/all_to_all | solution.py:124
  99.4 19.4 %all-to-all-start.5 = ((bf16[128,2,256]{2,1,0:T(2,128)(2,1)}), bf16[128,2,256]{2,1,0:T(2,128)(2,1)S(1)}, u32[]{:S(2)}, u32[]{:S(2)}) async-start(bf16[128,2,256]{2,1,0:T(2,128)(2,1)} %reshape.257), calls=%async_computation.5 | async-start | bytes 262144 | tf_op jit(solution)/shard_map/all_to_all | solution.py:127
  118.8 19.7 %all-to-all-start.1 = ((bf16[128,2,256]{2,1,0:T(2,128)(2,1)}), bf16[128,2,256]{2,1,0:T(2,128)(2,1)S(1)}, u32[]{:S(2)}, u32[]{:S(2)}) async-start(bf16[128,2,256]{2,1,0:T(2,128)(2,1)} %reshape.251), calls=%async_computation.1 | async-start | bytes 262144 | tf_op jit(solution)/shard_map/all_to_all | solution.py:130
  138.5 19.7 %all-to-all-start.2 = ((bf16[128,2,256]{2,1,0:T(2,128)(2,1)}), bf16[128,2,256]{2,1,0:T(2,128)(2,1)S(1)}, u32[]{:S(2)}, u32[]{:S(2)}) async-start(bf16[128,2,256]{2,1,0:T(2,128)(2,1)} %reshape.249), calls=%async_computation.2 | async-start | bytes 262144 | tf_op jit(solution)/shard_map/all_to_all | solution.py:133
  158.2 19.4 %all-to-all-start.11 = ((bf16[128,2,256]{2,1,0:T(2,128)(2,1)}), bf16[128,2,256]{2,1,0:T(2,128)(2,1)S(1)}, u32[]{:S(2)}, u32[]{:S(2)}) async-start(bf16[128,2,256]{2,1,0:T(2,128)(2,1)} %reshape.265), calls=%async_computation.11 | async-start | bytes 262144 | tf_op jit(solution)/shard_map/all_to_all | solution.py:121
  177.6 20.0 %all-to-all-start.10 = ((bf16[128,2,256]{2,1,0:T(2,128)(2,1)}), bf16[128,2,256]{2,1,0:T(2,128)(2,1)}, u32[]{:S(2)}, u32[]{:S(2)}) async-start(bf16[128,2,256]{2,1,0:T(2,128)(2,1)} %reshape.267), calls=%async_computation.10 | async-start | bytes 262144 | tf_op jit(solution)/shard_map/all_to_all | solution.py:118
  199.0 1.0 copy-start
  200.5 0.7 copy-start.4
  200.5 0.7 copy-start.5
  215.7 0.7 copy-start.9
  220.3 19.7 %all-to-all-start.12 = ((bf16[128,2,256]{2,1,0:T(2,128)(2,1)}), bf16[128,2,256]{2,1,0:T(2,128)(2,1)S(1)}, u32[]{:S(2)}, u32[]{:S(2)}) async-start(bf16[128,2,256]{2,1,0:T(2,128)(2,1)} %reshape.269), calls=%async_computation.12 | async-start | bytes 262144 | tf_op jit(solution)/shard_map/all_to_all | solution.py:156
  239.9 19.4 %all-to-all-start.13 = ((bf16[128,2,256]{2,1,0:T(2,128)(2,1)}), bf16[128,2,256]{2,1,0:T(2,128)(2,1)S(1)}, u32[]{:S(2)}, u32[]{:S(2)}) async-start(bf16[128,2,256]{2,1,0:T(2,128)(2,1)} %reshape.271), calls=%async_computation.13 | async-start | bytes 262144 | tf_op jit(solution)/shard_map/all_to_all | solution.py:159
  259.3 19.7 %all-to-all-start.6 = ((bf16[128,2,256]{2,1,0:T(2,128)(2,1)}), bf16[128,2,256]{2,1,0:T(2,128)(2,1)S(1)}, u32[]{:S(2)}, u32[]{:S(2)}) async-start(bf16[128,2,256]{2,1,0:T(2,128)(2,1)} %reshape.259), calls=%async_computation.6 | async-start | bytes 262144 | tf_op jit(solution)/shard_map/all_to_all | solution.py:150
  279.0 19.4 %all-to-all-start.7 = ((bf16[128,2,256]{2,1,0:T(2,128)(2,1)}), bf16[128,2,256]{2,1,0:T(2,128)(2,1)S(1)}, u32[]{:S(2)}, u32[]{:S(2)}) async-start(bf16[128,2,256]{2,1,0:T(2,128)(2,1)} %reshape.261), calls=%async_computation.7 | async-start | bytes 262144 | tf_op jit(solution)/shard_map/all_to_all | solution.py:153
  285.2 0.7 copy-start.8
  298.3 18.5 %all-to-all-start.14 = ((bf16[128,2,128]{2,1,0:T(2,128)(2,1)}), bf16[128,2,128]{2,1,0:T(2,128)(2,1)S(1)}, u32[]{:S(2)}, u32[]{:S(2)}) async-start(bf16[128,2,128]{2,1,0:T(2,128)(2,1)} %reshape.275), calls=%async_computation.14 | async-start | bytes 131072 | tf_op jit(solution)/shard_map/all_to_all | solution.py:169
  310.1 14.0 %copy-start.2 = (bf16[64,512]{1,0:T(8,128)(2,1)S(1)}, bf16[64,512]{1,0:T(8,128)(2,1)}, u32[]{:S(2)}) copy-start(bf16[64,512]{1,0:T(8,128)(2,1)} %param.5) | copy-start | bytes 196612
  316.8 18.9 %all-to-all-start.8 = ((bf16[128,2,128]{2,1,0:T(2,128)(2,1)}), bf16[128,2,128]{2,1,0:T(2,128)(2,1)S(1)}, u32[]{:S(2)}, u32[]{:S(2)}) async-start(bf16[128,2,128]{2,1,0:T(2,128)(2,1)} %reshape.273), calls=%async_computation.8 | async-start | bytes 131072 | tf_op jit(solution)/shard_map/all_to_all | solution.py:166
  324.0 0.8 copy-start.3
  324.0 337.9 %reduce-scatter.4.cloned.1.call-start = ((), (), s32[]{:S(2)}) async-start(), calls=%async_computation.16 | async-start | bytes 98304
  335.8 0.7 copy-start.10
Sparse Core Ops, SparseCore 0:
  327.3 15.6 reduce-scatter.3
where the time goes:
time: 680 us; the launch traced here: 671 us
  blocking collectives  324 us (48%)
  waiting for transfers between devices  142 us (21%)
  starting transfers between devices  111 us (16%)
  matrix products  39 us (6%)
  local copies, waits for them, and re-layouts  33.6 us (5%)
  between operations  15.7 us (2%)
    psum x1, blocking collectives, local(): skip_grad = lax.psum(local_skip, 'seq') * norm_factor  324 us
    unnamed x62, local copies, waits for them, and re-layouts  23.4 us
    all_to_all x1, starting transfers between devices, local(): lax.all_to_all(signal.reshape(channels, 1, length), 'seq', split_axis=2,...  16.4 us
  transfers between devices with their start and end apart: 16, of which 15 were waited for; matrix products, arithmetic and copies ran while one was open for 7% of the time, Pallas kernels for 0%

commit v1 on v0

--- a/solution.py
+++ b/solution.py
@@ -143,7 +143,7 @@
     corr_imag = signal_real * cotan_imag - signal_imag * cotan_real
     cotan_val = cotangent.astype(jnp.float32)
     local_skip = jnp.sum(cotan_val * signal.astype(jnp.float32), axis=1)
-    skip_grad = lax.psum(local_skip, "seq") * norm_factor
+    skip_grad = jnp.sum(lax.all_gather(local_skip, "seq"), axis=0) * norm_factor
     back_conv_real, back_conv_imag = local_inverse(conv_real, conv_imag)
     back_corr_real, back_corr_imag = local_inverse(corr_real, corr_imag)
     arrived = (

time: 680 us -> 999 us (1.47)
  blocking collectives: 324 us -> 638 us
    unnamed x0 -> x1, blocking collectives: none -> 638 us
    psum x1 -> x0, blocking collectives: 324 us -> none  [local(): skip_grad = lax.psum(local_skip, 'seq') * norm_factor]
    unnamed x62 -> x67, local copies, waits for them, and re-layouts: 23.4 us -> 24.9 us
  transfers between devices with their start and end apart: 16 -> 16, of which waited for: 15 -> 15; matrix products, arithmetic and copies ran while one was open for 7% -> 5% of each run, Pallas kernels for 0% -> 0%
where the time goes in v1:
time: 999 us; the launch traced here: 985 us
  blocking collectives  638 us (64%)
  waiting for transfers between devices  140 us (14%)
  starting transfers between devices  111 us (11%)
  matrix products  38.9 us (4%)
  local copies, waits for them, and re-layouts  35.1 us (4%)
  between operations  16.1 us (2%)
    unnamed x1, blocking collectives  638 us
    unnamed x67, local copies, waits for them, and re-layouts  24.9 us
  transfers between devices with their start and end apart: 16, of which 15 were waited for; matrix products, arithmetic and copies ran while one was open for 5% of the time, Pallas kernels for 0%

profile of v1, /device:TPU:1, one launch (start us, length us, event | category | flops | bytes accessed | tf_op | source)
XLA Modules:
  0.0 984.6 jit_solution(8295630386276611391)
XLA Ops:
  7.2 1.0 copy.333
  8.7 1.4 reduce
  10.9 16.4 %all-to-all-start.9 = ((bf16[128,2,128]{2,1,0:T(2,128)(2,1)}), bf16[128,2,128]{2,1,0:T(2,128)(2,1)S(1)}, u32[]{:S(2)}, u32[]{:S(2)}) async-start(bf16[128,2,128]{2,1,0:T(2,128)(2,1)} %reshape.269), calls=%async_computation.9 | async-start | bytes 131072 | tf_op jit(solution)/shard_map/all_to_all | solution.py:102
  28.3 1.5 reduce.1
  30.8 1.5 reduce.2
  33.2 5.8 all-to-all-done.9
  39.0 8.0 all-to-all-start.3
  48.8 9.9 %all-to-all-done.3 = bf16[128,2,128]{2,1,0:T(2,128)(2,1)S(1)} async-done(((bf16[128,2,128]{2,1,0:T(2,128)(2,1)}), bf16[128,2,128]{2,1,0:T(2,128)(2,1)S(1)}, u32[]{:S(2)}, u32[]{:S(2)}) %all-to-all-start.3) | async-done | bytes 65568 | tf_op jit(solution)/shard_map/all_to_all | solution.py:105
  58.7 6.5 all-to-all-start
  67.0 10.0 %all-to-all-done = bf16[128,2,128]{2,1,0:T(2,128)(2,1)S(1)} async-done(((bf16[128,2,128]{2,1,0:T(2,128)(2,1)}), bf16[128,2,128]{2,1,0:T(2,128)(2,1)S(1)}, u32[]{:S(2)}, u32[]{:S(2)}) %all-to-all-start) | async-done | bytes 65568 | tf_op jit(solution)/shard_map/all_to_all | solution.py:108
  78.1 0.9 fusion.97
  79.2 0.9 reshape.261
  80.0 6.3 all-to-all-start.4
  86.5 0.9 reshape.263
  87.3 12.1 %all-to-all-done.4 = bf16[128,2,256]{2,1,0:T(2,128)(2,1)S(1)} async-done(((bf16[128,2,256]{2,1,0:T(2,128)(2,1)}), bf16[128,2,256]{2,1,0:T(2,128)(2,1)S(1)}, u32[]{:S(2)}, u32[]{:S(2)}) %all-to-all-start.4) | async-done | bytes 131104 | tf_op jit(solution)/shard_map/all_to_all | solution.py:124
  99.4 6.3 all-to-all-start.5
  106.5 0.9 reshape.257
  107.4 11.4 %all-to-all-done.5 = bf16[128,2,256]{2,1,0:T(2,128)(2,1)S(1)} async-done(((bf16[128,2,256]{2,1,0:T(2,128)(2,1)}), bf16[128,2,256]{2,1,0:T(2,128)(2,1)S(1)}, u32[]{:S(2)}, u32[]{:S(2)}) %all-to-all-start.5) | async-done | bytes 131104 | tf_op jit(solution)/shard_map/all_to_all | solution.py:127
  118.8 6.6 all-to-all-start.1
  127.0 0.9 reshape.255
  128.1 0.9 reshape.271
  129.1 0.9 reshape.273
  131.3 7.1 all-to-all-done.1
  138.4 6.8 all-to-all-start.2
  147.0 11.2 %all-to-all-done.2 = bf16[128,2,256]{2,1,0:T(2,128)(2,1)S(1)} async-done(((bf16[128,2,256]{2,1,0:T(2,128)(2,1)}), bf16[128,2,256]{2,1,0:T(2,128)(2,1)S(1)}, u32[]{:S(2)}, u32[]{:S(2)}) %all-to-all-start.2) | async-done | bytes 131104 | tf_op jit(solution)/shard_map/all_to_all | solution.py:133
  158.2 6.3 all-to-all-start.11
  165.8 11.8 %all-to-all-done.11 = bf16[128,2,256]{2,1,0:T(2,128)(2,1)S(1)} async-done(((bf16[128,2,256]{2,1,0:T(2,128)(2,1)}), bf16[128,2,256]{2,1,0:T(2,128)(2,1)S(1)}, u32[]{:S(2)}, u32[]{:S(2)}) %all-to-all-start.11) | async-done | bytes 131104 | tf_op jit(solution)/shard_map/all_to_all | solution.py:121
  177.6 7.7 all-to-all-start.10
  185.8 1.2 convolution_multiply_fusion.1
  187.4 10.2 %all-to-all-done.10 = bf16[128,2,256]{2,1,0:T(2,128)(2,1)} async-done(((bf16[128,2,256]{2,1,0:T(2,128)(2,1)}), bf16[128,2,256]{2,1,0:T(2,128)(2,1)}, u32[]{:S(2)}, u32[]{:S(2)}) %all-to-all-start.10) | async-done | bytes 131104 | tf_op jit(solution)/shard_map/all_to_all | solution.py:118
  197.6 1.1 reshape.274
  208.9 0.8 fusion.1
  210.5 1.2 multiply_subtract_fusion.1
  216.4 0.9 multiply_subtract_fusion
  217.2 0.8 fusion.38
  218.1 0.9 fusion.11
  219.3 0.9 reshape.275
  220.2 6.6 all-to-all-start.12
  226.8 0.8 fusion.34
  227.6 0.9 fusion.10
  228.9 0.9 reshape.277
  229.7 10.1 %all-to-all-done.12 = bf16[128,2,256]{2,1,0:T(2,128)(2,1)S(1)} async-done(((bf16[128,2,256]{2,1,0:T(2,128)(2,1)}), bf16[128,2,256]{2,1,0:T(2,128)(2,1)S(1)}, u32[]{:S(2)}, u32[]{:S(2)}) %all-to-all-start.12) | async-done | bytes 131104 | tf_op jit(solution)/shard_map/all_to_all | solution.py:156
  239.8 6.3 all-to-all-start.13
  246.1 0.8 fusion.50
  247.0 0.9 fusion.13
  248.2 0.9 reshape.265
  249.0 10.2 %all-to-all-done.13 = bf16[128,2,256]{2,1,0:T(2,128)(2,1)S(1)} async-done(((bf16[128,2,256]{2,1,0:T(2,128)(2,1)}), bf16[128,2,256]{2,1,0:T(2,128)(2,1)S(1)}, u32[]{:S(2)}, u32[]{:S(2)}) %all-to-all-start.13) | async-done | bytes 131104 | tf_op jit(solution)/shard_map/all_to_all | solution.py:159
  259.2 6.8 all-to-all-start.6
  266.0 0.8 fusion.46
  266.8 0.9 fusion.12
  268.1 0.9 reshape.267
  270.8 8.2 all-to-all-done.6
  279.0 6.3 all-to-all-start.7
  285.9 1.5 fusion.23
  287.5 1.5 fusion.18
  290.9 7.5 all-to-all-done.7
  298.4 6.6 all-to-all-start.14
  306.0 1.5 fusion.30
  307.5 1.5 fusion.19
  310.0 6.8 all-to-all-done.14
  316.8 7.2 all-to-all-start.8
  327.7 7.9 all-to-all-done.8
  336.7 637.8 %all-reduce = f32[8192]{0:T(1024)S(1)} all-reduce(f32[8192]{0:T(1024)S(1)} %dynamic-update-slice), channel_id=2, replica_groups=mesh['seq'=128,'chan'=2] {'seq'}, use_global_device_ids=true, to_apply=%add | all-reduce | flops 8192 | bytes 65536
  975.9 0.9 copy.379
  (152 shorter events, 46.0 us)
Async XLA Ops:
  10.9 28.1 %all-to-all-start.9 = ((bf16[128,2,128]{2,1,0:T(2,128)(2,1)}), bf16[128,2,128]{2,1,0:T(2,128)(2,1)S(1)}, u32[]{:S(2)}, u32[]{:S(2)}) async-start(bf16[128,2,128]{2,1,0:T(2,128)(2,1)} %reshape.269), calls=%async_computation.9 | async-start | bytes 131072 | tf_op jit(solution)/shard_map/all_to_all | solution.py:102
  27.3 0.8 copy-start.1
  27.6 50.5 %copy-start.7 = (s32[256]{0:T(256)}, s32[256]{0:T(256)S(1)}, u32[]{:S(2)}) copy-start(s32[256]{0:T(256)S(1)} %mul.1168) | copy-start | bytes 3076
  29.8 0.8 copy-start.6
  39.0 19.7 %all-to-all-start.3 = ((bf16[128,2,128]{2,1,0:T(2,128)(2,1)}), bf16[128,2,128]{2,1,0:T(2,128)(2,1)S(1)}, u32[]{:S(2)}, u32[]{:S(2)}) async-start(bf16[128,2,128]{2,1,0:T(2,128)(2,1)} %reshape.259), calls=%async_computation.3 | async-start | bytes 131072 | tf_op jit(solution)/shard_map/all_to_all | solution.py:105
  58.7 18.4 %all-to-all-start = ((bf16[128,2,128]{2,1,0:T(2,128)(2,1)}), bf16[128,2,128]{2,1,0:T(2,128)(2,1)S(1)}, u32[]{:S(2)}, u32[]{:S(2)}) async-start(bf16[128,2,128]{2,1,0:T(2,128)(2,1)} %reshape.253), calls=%async_computation | async-start | bytes 131072 | tf_op jit(solution)/shard_map/all_to_all | solution.py:108
  80.0 19.4 %all-to-all-start.4 = ((bf16[128,2,256]{2,1,0:T(2,128)(2,1)}), bf16[128,2,256]{2,1,0:T(2,128)(2,1)S(1)}, u32[]{:S(2)}, u32[]{:S(2)}) async-start(bf16[128,2,256]{2,1,0:T(2,128)(2,1)} %reshape.261), calls=%async_computation.4 | async-start | bytes 262144 | tf_op jit(solution)/shard_map/all_to_all | solution.py:124
  99.4 19.4 %all-to-all-start.5 = ((bf16[128,2,256]{2,1,0:T(2,128)(2,1)}), bf16[128,2,256]{2,1,0:T(2,128)(2,1)S(1)}, u32[]{:S(2)}, u32[]{:S(2)}) async-start(bf16[128,2,256]{2,1,0:T(2,128)(2,1)} %reshape.263), calls=%async_computation.5 | async-start | bytes 262144 | tf_op jit(solution)/shard_map/all_to_all | solution.py:127
  118.8 19.7 %all-to-all-start.1 = ((bf16[128,2,256]{2,1,0:T(2,128)(2,1)}), bf16[128,2,256]{2,1,0:T(2,128)(2,1)S(1)}, u32[]{:S(2)}, u32[]{:S(2)}) async-start(bf16[128,2,256]{2,1,0:T(2,128)(2,1)} %reshape.257), calls=%async_computation.1 | async-start | bytes 262144 | tf_op jit(solution)/shard_map/all_to_all | solution.py:130
  138.4 19.7 %all-to-all-start.2 = ((bf16[128,2,256]{2,1,0:T(2,128)(2,1)}), bf16[128,2,256]{2,1,0:T(2,128)(2,1)S(1)}, u32[]{:S(2)}, u32[]{:S(2)}) async-start(bf16[128,2,256]{2,1,0:T(2,128)(2,1)} %reshape.255), calls=%async_computation.2 | async-start | bytes 262144 | tf_op jit(solution)/shard_map/all_to_all | solution.py:133
  158.2 19.4 %all-to-all-start.11 = ((bf16[128,2,256]{2,1,0:T(2,128)(2,1)}), bf16[128,2,256]{2,1,0:T(2,128)(2,1)S(1)}, u32[]{:S(2)}, u32[]{:S(2)}) async-start(bf16[128,2,256]{2,1,0:T(2,128)(2,1)} %reshape.271), calls=%async_computation.11 | async-start | bytes 262144 | tf_op jit(solution)/shard_map/all_to_all | solution.py:121
  177.6 20.1 %all-to-all-start.10 = ((bf16[128,2,256]{2,1,0:T(2,128)(2,1)}), bf16[128,2,256]{2,1,0:T(2,128)(2,1)}, u32[]{:S(2)}, u32[]{:S(2)}) async-start(bf16[128,2,256]{2,1,0:T(2,128)(2,1)} %reshape.273), calls=%async_computation.10 | async-start | bytes 262144 | tf_op jit(solution)/shard_map/all_to_all | solution.py:118
  199.0 1.0 copy-start
  200.5 0.7 copy-start.4
  200.5 0.7 copy-start.5
  215.7 0.7 copy-start.9
  220.2 19.7 %all-to-all-start.12 = ((bf16[128,2,256]{2,1,0:T(2,128)(2,1)}), bf16[128,2,256]{2,1,0:T(2,128)(2,1)S(1)}, u32[]{:S(2)}, u32[]{:S(2)}) async-start(bf16[128,2,256]{2,1,0:T(2,128)(2,1)} %reshape.275), calls=%async_computation.12 | async-start | bytes 262144 | tf_op jit(solution)/shard_map/all_to_all | solution.py:156
  239.8 19.4 %all-to-all-start.13 = ((bf16[128,2,256]{2,1,0:T(2,128)(2,1)}), bf16[128,2,256]{2,1,0:T(2,128)(2,1)S(1)}, u32[]{:S(2)}, u32[]{:S(2)}) async-start(bf16[128,2,256]{2,1,0:T(2,128)(2,1)} %reshape.277), calls=%async_computation.13 | async-start | bytes 262144 | tf_op jit(solution)/shard_map/all_to_all | solution.py:159
  259.2 19.8 %all-to-all-start.6 = ((bf16[128,2,256]{2,1,0:T(2,128)(2,1)}), bf16[128,2,256]{2,1,0:T(2,128)(2,1)S(1)}, u32[]{:S(2)}, u32[]{:S(2)}) async-start(bf16[128,2,256]{2,1,0:T(2,128)(2,1)} %reshape.265), calls=%async_computation.6 | async-start | bytes 262144 | tf_op jit(solution)/shard_map/all_to_all | solution.py:150
  279.0 19.4 %all-to-all-start.7 = ((bf16[128,2,256]{2,1,0:T(2,128)(2,1)}), bf16[128,2,256]{2,1,0:T(2,128)(2,1)S(1)}, u32[]{:S(2)}, u32[]{:S(2)}) async-start(bf16[128,2,256]{2,1,0:T(2,128)(2,1)} %reshape.267), calls=%async_computation.7 | async-start | bytes 262144 | tf_op jit(solution)/shard_map/all_to_all | solution.py:153
  285.3 0.6 copy-start.8
  298.4 18.4 %all-to-all-start.14 = ((bf16[128,2,128]{2,1,0:T(2,128)(2,1)}), bf16[128,2,128]{2,1,0:T(2,128)(2,1)S(1)}, u32[]{:S(2)}, u32[]{:S(2)}) async-start(bf16[128,2,128]{2,1,0:T(2,128)(2,1)} %reshape.281), calls=%async_computation.14 | async-start | bytes 131072 | tf_op jit(solution)/shard_map/all_to_all | solution.py:169
  309.9 14.0 %copy-start.2 = (bf16[64,512]{1,0:T(8,128)(2,1)S(1)}, bf16[64,512]{1,0:T(8,128)(2,1)}, u32[]{:S(2)}) copy-start(bf16[64,512]{1,0:T(8,128)(2,1)} %param.5) | copy-start | bytes 196612
  316.8 18.8 %all-to-all-start.8 = ((bf16[128,2,128]{2,1,0:T(2,128)(2,1)}), bf16[128,2,128]{2,1,0:T(2,128)(2,1)S(1)}, u32[]{:S(2)}, u32[]{:S(2)}) async-start(bf16[128,2,128]{2,1,0:T(2,128)(2,1)} %reshape.279), calls=%async_computation.8 | async-start | bytes 131072 | tf_op jit(solution)/shard_map/all_to_all | solution.py:166
  323.9 0.8 copy-start.3
  323.9 652.0 %reduce-scatter.4.cloned.1.call-start = ((), (), s32[]{:S(2)}) async-start(), calls=%async_computation.16 | async-start | bytes 98304
  324.9 0.7 copy-start.11
  335.7 0.7 copy-start.10
Sparse Core Ops, SparseCore 0:
  327.8 15.6 reduce-scatter.3
